TPU v7x, 128 devices: a whole 4x4x4 slice. The times are simulated.
128 devices in a mesh: aux: 32 (over z, x, y_lo), pair: 4 (over y_hi, core).
Axes of the slice: x: 4, y: 4 (y_hi: 2, y_lo: 2; y = y_hi * 2 + y_lo), z: 4, core: 2. Of those that a mesh axis runs over, the one named last changes fastest.
Arguments:
- ia_aux: bfloat16 [16384, 24576], P('pair', 'aux'), may hold values from -0.15625 to 0.15625
- occ_block: int32 [4], replicated, may hold values from 0 to 149
- virt_block: int32 [4], replicated, may hold values from 0 to 19
- owners: int32 [2], replicated, may hold values from 0 to 31
- occ_energy: float32 [1200], replicated, may hold values from -2.5 to -0.4
- virt_energy: float32 [10240], replicated, may hold values from 0.2 to 4
Outputs:
- row_energy: float32 [16384], P(('pair', 'aux'))
- mean_energy: float32 [], replicated
All inputs are finite; a program needn't handle non-finite values.
Results may differ from a plain program's by a relative error of at most 0.0003.
Values may be sent and summed in bfloat16 or wider, within the bound.
A program may use at most 128 MiB of HBM per device.

v0:
```python
import jax
import jax.numpy as jnp
from jax import lax
from jax.sharding import PartitionSpec as P

OB = 8
VB = 512
STEPS = 2


spin_scale = 1.3


def broadcast(block, axis, owner):
    block = jnp.where(lax.axis_index(axis) == owner, block, jnp.zeros_like(block))
    return lax.psum(block, axis)


def row_gaps(first_row, row_count, occ_block, virt_block, occ_energy, virt_energy):
    row_index = first_row + jnp.arange(row_count, dtype=jnp.int32)
    per_block = OB * VB
    block_index = row_index // per_block
    within_block = row_index % per_block
    occ_index = jnp.take(occ_block, block_index) * OB + within_block // VB
    virt_index = jnp.take(virt_block, block_index) * VB + within_block % VB
    return jnp.take(virt_energy, virt_index) - jnp.take(occ_energy, occ_index)


def pair_terms(intersection, own_gaps, partner_gaps):
    return jnp.sum(
        intersection * intersection / (own_gaps[:, None] + partner_gaps[None, :]), axis=1
    )


def shards(ia_aux, occ_block, virt_block, owners, occ_energy, virt_energy):
    aux_count = lax.axis_size("aux")
    aux_index = lax.axis_index("aux")
    pair_index = lax.axis_index("pair")
    slice_rows = ia_aux.shape[0]
    group_rows = slice_rows // aux_count
    group_base = pair_index * aux_count
    own_first = (group_base + aux_index) * group_rows
    own_gaps = row_gaps(own_first, group_rows, occ_block, virt_block, occ_energy, virt_energy)
    partner_gaps = [
        row_gaps(
            (group_base + owners[turn_index]) * group_rows,
            group_rows,
            occ_block,
            virt_block,
            occ_energy,
            virt_energy,
        )
        for turn_index in range(STEPS)
    ]
    totals = jnp.zeros((group_rows,), jnp.float32)
    own_block = lax.all_to_all(ia_aux, "aux", split_axis=0, concat_axis=1, tiled=True)
    for turn_index in range(STEPS):
        partner = broadcast(own_block, "aux", owners[turn_index])
        intersection = lax.dot_general(
            own_block, partner, (((1,), (1,)), ((), ())), preferred_element_type=jnp.float32
        )
        totals = totals + pair_terms(intersection, own_gaps, partner_gaps[turn_index])
    row_energy = -spin_scale * totals
    window_total = lax.psum(jnp.sum(row_energy), ("aux", "pair"))
    mean_energy = window_total / (slice_rows * lax.axis_size("pair"))
    return (row_energy, mean_energy)


def solution(mesh):
    placed = (P("pair", "aux"), P(), P(), P(), P(), P())
    return jax.shard_map(
        shards, mesh=mesh, in_specs=placed, out_specs=(P(("pair", "aux")), P()), check_vma=False
    )
```

profile of v0, /device:TPU:1, one launch (start us, length us, event | category | flops | bytes accessed | tf_op | source)
XLA Modules:
  0.0 758.4 jit_solution(11412868367658027417)
XLA Ops:
  7.2 10.0 %all-to-all-start = ((bf16[32,128,768]{2,1,0:T(8,128)(2,1)}), bf16[32,128,768]{2,1,0:T(8,128)(2,1)}, u32[]{:S(2)}, u32[]{:S(2)}) async-start(bf16[32,128,768]{2,1,0:T(8,128)(2,1)} %bitcast.51), calls=%async_computation | async-start | bytes 12582912 | tf_op jit(solution)/shard_map/all_to_all | solution.py:56
  17.2 0.0 all-reduce.3.cloned.1.call-start
  17.2 0.6 fusion.21
  19.1 80.8 %all-to-all-done = bf16[32,128,768]{2,1,0:T(8,128)(2,1)} async-done(((bf16[32,128,768]{2,1,0:T(8,128)(2,1)}), bf16[32,128,768]{2,1,0:T(8,128)(2,1)}, u32[]{:S(2)}, u32[]{:S(2)}) %all-to-all-start) | async-done | bytes 6291488 | tf_op jit(solution)/shard_map/all_to_all | solution.py:56
  99.9 8.6 %copy.8 = bf16[128,32,768]{0,2,1:T(8,128)(2,1)} copy(bf16[128,32,768]{2,0,1:T(8,128)(2,1)} %bitcast.2) | data formatting | bytes 12582912 | tf_op jit(solution)/shard_map/all_to_all | solution.py:56
  108.5 7.4 broadcast_select_fusion
  115.9 0.0 all-reduce.3.cloned.1.call-update
  117.3 0.7 fusion.19
  117.9 0.7 fusion.20
  118.6 5.2 compare_select_fusion.6
  123.8 1.1 gather_fusion
  125.0 2.5 compare_select_fusion.1
  127.5 1.1 gather_fusion.4
  128.6 1.1 gather_fusion.2
  129.8 1.1 gather_fusion.1
  131.0 2.7 compare_select_fusion
  133.7 1.1 gather_fusion.5
  134.9 1.1 gather_fusion.3
  136.1 539.5 %all-reduce.3.cloned.1.call-done = (bf16[128,24576]{0,1:T(8,128)(2,1)}, bf16[128,24576]{0,1:T(8,128)(2,1)}) async-done(((bf16[128,24576]{0,1:T(8,128)(2,1)}, bf16[128,24576]{0,1:T(8,128)(2,1)}), (bf16[128,24576]{0,1:T(8,128)(2,1)}, bf16[128,24576]{0,1:T(8,128)(2,1)})) %all-reduce.3.cloned.1.call-update) | async-done | bytes 12582928 | tf_op jit(solution)/shard_map/psum | solution.py:16
  675.6 6.6 fusion.4
  682.2 1.0 copy-done.2
  683.3 1.9 fusion.5
  685.1 1.1 fusion.18
  686.2 63.5 %psum.23 = f32[]{:T(128)} all-reduce(f32[]{:T(128)} %get-tuple-element.7), channel_id=1, replica_groups=mesh['aux'=32,'pair'=4] {'aux','pair'}, use_global_device_ids=true, to_apply=%region_5.9 | all-reduce | flops 1 | bytes 8 | tf_op jit(solution)/shard_map/psum | solution.py:64
  (25 shorter events, 0.1 us)
Async XLA Ops:
  7.2 116.6 %copy-start = (f32[10240]{0:T(1024)S(1)}, f32[10240]{0:T(1024)}, u32[]{:S(2)}) copy-start(f32[10240]{0:T(1024)} %param.17) | copy-start | bytes 122884
  7.2 10.1 %copy-start.5 = (s32[2]{0:T(128)S(1)}, s32[2]{0:T(128)}, u32[]{:S(2)}) copy-start(s32[2]{0:T(128)} %param.15) | copy-start | bytes 28
  7.2 92.7 %all-to-all-start = ((bf16[32,128,768]{2,1,0:T(8,128)(2,1)}), bf16[32,128,768]{2,1,0:T(8,128)(2,1)}, u32[]{:S(2)}, u32[]{:S(2)}) async-start(bf16[32,128,768]{2,1,0:T(8,128)(2,1)} %bitcast.51), calls=%async_computation | async-start | bytes 12582912 | tf_op jit(solution)/shard_map/all_to_all | solution.py:56
  17.2 658.4 %all-reduce.3.cloned.1.call-start = ((), (), s32[]{:S(2)}) async-start(), calls=%async_computation.1 | async-start | bytes 25165824 | tf_op jit(solution)/shard_map/psum | solution.py:16
  115.9 1.4 copy-start.3
  115.9 2.0 copy-start.4
  115.9 13.9 %copy-start.1 = (f32[1200]{0:T(1024)S(1)}, f32[1200]{0:T(1024)}, u32[]{:S(2)}) copy-start(f32[1200]{0:T(1024)} %param.16) | copy-start | bytes 14404
  133.7 548.5 %slice-start = ((s8[6291456]{0:T(1024)(128)(4,1)}), s8[2097152]{0:T(1024)(128)(4,1)S(1)}, s32[]{:S(2)}) async-start(s8[6291456]{0:T(1024)(128)(4,1)} %bitcast.48), calls=%async_computation.2 | async-start | bytes 4194304
  675.6 6.6 slice-start.1
  675.6 7.7 %copy-start.2 = (bf16[128,24576]{0,1:T(8,128)(2,1)S(1)}, bf16[128,24576]{0,1:T(8,128)(2,1)}, u32[]{:S(2)}) copy-start(bf16[128,24576]{0,1:T(8,128)(2,1)} %get-tuple-element.6) | copy-start | bytes 18874372
Sparse Core Ops, SparseCore 0:
  116.1 559.4 all-reduce.2
where the time goes:
time: 759 us; the launch traced here: 758 us
  waiting for transfers between devices  620 us (82%)
  blocking collectives  63.5 us (8%)
  other arithmetic  19 us (3%)
  between operations  18.7 us (2%)
  local copies, waits for them, and re-layouts  18.5 us (2%)
  starting transfers between devices  10 us (1%)
  matrix products  8.46 us (1%)
    psum x1, waiting for transfers between devices, broadcast(): return lax.psum(block, axis)  539 us
    all_to_all x1, waiting for transfers between devices, shards(): lax.all_to_all(ia_aux, 'aux', split_axis=0, concat_axis=1, tiled=True)  80.8 us
    psum x1, blocking collectives, shards(): window_total = lax.psum(jnp.sum(row_energy), ('aux', 'pair'))  63.5 us
  transfers between devices with their start and end apart: 2, of which 2 were waited for; matrix products, arithmetic and copies ran while one was open for 3% of the time, Pallas kernels for 0%

commit v1 on v0

v1 whole, which is shorter than its diff:
```python
import jax
import jax.numpy as jnp
from jax import lax
from jax.sharding import PartitionSpec as P

OB = 8
VB = 512
STEPS = 2


spin_scale = 1.3


def row_gaps(first_row, row_count, occ_block, virt_block, occ_energy, virt_energy):
    per_block = OB * VB
    block_index = first_row // per_block
    within_block = first_row % per_block
    occ_index = occ_block[block_index] * OB + within_block // VB
    virt_index = virt_block[block_index] * VB + within_block % VB
    return lax.dynamic_slice_in_dim(virt_energy, virt_index, row_count) - occ_energy[occ_index]


def shards(ia_aux, occ_block, virt_block, owners, occ_energy, virt_energy):
    aux_count = lax.axis_size("aux")
    aux_index = lax.axis_index("aux")
    pair_index = lax.axis_index("pair")
    slice_rows = ia_aux.shape[0]
    group_rows = slice_rows // aux_count
    group_base = pair_index * aux_count
    tables = (occ_block, virt_block, occ_energy, virt_energy)
    own_gaps = row_gaps((group_base + aux_index) * group_rows, group_rows, *tables)
    partner_gaps = jnp.concatenate(
        [row_gaps((group_base + owners[t]) * group_rows, group_rows, *tables) for t in range(STEPS)]
    )
    partners = jnp.concatenate(
        [
            lax.dynamic_slice_in_dim(ia_aux, owners[t] * group_rows, group_rows, 0)
            for t in range(STEPS)
        ]
    )
    partial = lax.dot_general(
        ia_aux, partners, (((1,), (1,)), ((), ())), preferred_element_type=jnp.float32
    )
    intersection = lax.psum_scatter(partial, "aux", scatter_dimension=0, tiled=True)
    totals = jnp.sum(
        intersection * intersection / (own_gaps[:, None] + partner_gaps[None, :]), axis=1
    )
    row_energy = -spin_scale * totals
    window_total = lax.psum(jnp.sum(row_energy), ("aux", "pair"))
    mean_energy = window_total / (slice_rows * lax.axis_size("pair"))
    return (row_energy, mean_energy)


def solution(mesh):
    placed = (P("pair", "aux"), P(), P(), P(), P(), P())
    return jax.shard_map(
        shards, mesh=mesh, in_specs=placed, out_specs=(P(("pair", "aux")), P()), check_vma=False
    )
```

time: 759 us -> 264 us (0.35)
  waiting for transfers between devices: 620 us -> 139 us
  blocking collectives: 63.5 us -> 85.5 us
  other arithmetic: 19 us -> 4.94 us
  local copies, waits for them, and re-layouts: 18.5 us -> 4.48 us
  starting transfers between devices: 10 us -> 0.04 us
    psum x1 -> x0, waiting for transfers between devices: 539 us -> none  [broadcast(): return lax.psum(block, axis)]
    reduce_scatter x0 -> x1, waiting for transfers between devices: none -> 139 us  [shards(): lax.psum_scatter(partial, 'aux', scatter_dimension=0, tiled=True)]
    all_to_all x1 -> x0, waiting for transfers between devices: 80.8 us -> none  [shards(): lax.all_to_all(ia_aux, 'aux', split_axis=0, concat_axis=1, tiled=True)]
    psum x1, blocking collectives: 63.5 us -> 85.5 us  [shards(): window_total = lax.psum(jnp.sum(row_energy), ('aux', 'pair'))]
    select_n x4 -> x0, other arithmetic: 17.8 us -> none  [the longest x3 10.4 us: row_gaps(): return jnp.take(virt_energy, virt_index) - jnp.take(occ_energy, occ_index)]
    all_to_all x1 -> x0, starting transfers between devices: 9.98 us -> none  [shards(): lax.all_to_all(ia_aux, 'aux', split_axis=0, concat_axis=1, tiled=True)]
    all_to_all x1 -> x0, local copies, waits for them, and re-layouts: 8.62 us -> none  [shards(): lax.all_to_all(ia_aux, 'aux', split_axis=0, concat_axis=1, tiled=True)]
    gather x8 -> x0, local copies, waits for them, and re-layouts: 8.21 us -> none  [the longest x6 6.89 us: row_gaps(): return jnp.take(virt_energy, virt_index) - jnp.take(occ_energy, occ_index)]
  transfers between devices with their start and end apart: 2 -> 1, of which waited for: 2 -> 1; matrix products, arithmetic and copies ran while one was open for 3% -> 2% of each run, Pallas kernels for 0% -> 0%
where the time goes in v1:
time: 264 us; the launch traced here: 263 us
  waiting for transfers between devices  139 us (53%)
  blocking collectives  85.5 us (32%)
  between operations  22.4 us (8%)
  matrix products  6.57 us (2%)
  other arithmetic  4.94 us (2%)
  local copies, waits for them, and re-layouts  4.48 us (2%)
    reduce_scatter x1, waiting for transfers between devices, shards(): lax.psum_scatter(partial, 'aux', scatter_dimension=0, tiled=True)  139 us
    psum x1, blocking collectives, shards(): window_total = lax.psum(jnp.sum(row_energy), ('aux', 'pair'))  85.5 us
    dot_general x1, matrix products, shards(): lax.dot_general(ia_aux, partners, (((1,), (1,)), ((), ())), preferred_ele...  6.57 us
  transfers between devices with their start and end apart: 1, of which 1 were waited for; matrix products, arithmetic and copies ran while one was open for 2% of the time, Pallas kernels for 0%

profile of v1, /device:TPU:1, one launch (start us, length us, event | category | flops | bytes accessed | tf_op | source)
XLA Modules:
  0.0 263.3 jit_solution(607822628051124859)
XLA Ops:
  7.2 0.0 reduce-scatter.2.cloned.1.call-start
  7.2 1.3 fusion.9
  9.8 1.1 constant_dynamic-slice_fusion.1
  10.9 0.0 copy-start
  10.9 0.0 copy-start.1
  10.9 6.6 %convolution_bitcast_fusion = f32[4096,256]{0,1:T(8,128)} fusion(bf16[4096,768]{1,0:T(8,128)(2,1)} %param.6, bf16[128,768]{1,0:T(8,128)(2,1)S(1)} %get-tuple-element.5, bf16[128,768]{1,0:T(8,128)(2,1)S(1)} %get-tuple-element.4), kind=kOutput, calls=%fused_computation | convolution fusion | flops 1611399168 | bytes 10878976 | tf_op jit(solution)/shard_map/dot_general | solution.py:41
  17.5 0.0 reduce-scatter.2.cloned.1.call-update
  18.9 0.0 copy-done
  18.9 0.0 copy-done.1
  18.9 0.7 fusion.7
  23.5 1.4 fusion.6
  24.9 2.8 %dynamic-slice_subtract_fusion.2 = (f32[128]{0:T(128)S(1)}, f32[128]{0:T(128)S(1)}, f32[128]{0:T(128)S(1)}) fusion(f32[10240]{0:T(1024)} %param.11, s32[]{:T(128)S(6)} %select_n.88, f32[]{:T(128)} %bitcast.5, f32[]{:T(128)} %bitcast.11, s32[]{:T(128)S(6)} %select_n.102, f32[]{:T(128)} %bitcast.8, s32[]{:T(128)S(6)} %select_n.95), kind=kLoop, calls=%fused_computation.9 | loop fusion | flops 384 | bytes 3096 | tf_op jit(solution)/shard_map/sub | solution.py:20
  27.7 139.3 %reduce-scatter.2.cloned.1.call-done = f32[128,256]{0,1:T(8,128)} async-done(((f32[4096,256]{0,1:T(8,128)}), f32[128,256]{0,1:T(8,128)}) %reduce-scatter.2.cloned.1.call-update) | async-done | bytes 131088 | tf_op jit(solution)/shard_map/reduce_scatter | solution.py:44
  167.0 1.0 fusion.3
  168.0 1.1 fusion.5
  169.2 85.5 %psum.7 = f32[]{:T(128)} all-reduce(f32[]{:T(128)} %get-tuple-element.2), channel_id=1, replica_groups=mesh['aux'=32,'pair'=4] {'aux','pair'}, use_global_device_ids=true, to_apply=%region_3.4 | all-reduce | flops 1 | bytes 8 | tf_op jit(solution)/shard_map/psum | solution.py:49
  (1 shorter events, 0.0 us)
Async XLA Ops:
  7.2 159.8 %reduce-scatter.2.cloned.1.call-start = ((), (), s32[]{:S(2)}) async-start(), calls=%async_computation.1 | async-start | bytes 4325376 | tf_op jit(solution)/shard_map/reduce_scatter | solution.py:44
  10.9 8.0 %copy-start = (s32[4]{0:T(128)S(1)}, s32[4]{0:T(128)}, u32[]{:S(2)}) copy-start(s32[4]{0:T(128)} %param.7) | copy-start | bytes 52
  10.9 8.0 %copy-start.1 = (s32[4]{0:T(128)S(1)}, s32[4]{0:T(128)}, u32[]{:S(2)}) copy-start(s32[4]{0:T(128)} %param.8) | copy-start | bytes 52
Sparse Core Ops, SparseCore 0:
  17.6 149.3 reduce-scatter.1

commit v2 on v1

v2 whole, which is shorter than its diff:
```python
import itertools

import jax
import jax.numpy as jnp
from jax import lax
from jax.experimental import pallas as pl
from jax.experimental.pallas import tpu as pltpu
from jax.sharding import PartitionSpec as P

OB = 8
VB = 512
STEPS = 2
GROUP = 128
GROUPS = 32
HALF = GROUP // 2
WIDE = STEPS * GROUP
DEPTH = 768
TOP = 32764.0

MESH = pl.DeviceIdType.MESH
spin_scale = 1.3

FIRST_PEERS = [s for s in itertools.product((0,), range(4), (0,), (0,), range(2)) if any(s)]
SECOND_PEERS = [s for s in itertools.product(range(4), (0,), range(2), range(2), (0,)) if any(s)]


def encode(v, out):
    n = v.shape[0] // 16
    v = v.reshape(n, 16, WIDE)
    top = jnp.max(jnp.abs(v), axis=0)
    power = jnp.ceil(jnp.log2(jnp.maximum(top, 1e-30)))
    q = jnp.round(v * (jnp.exp2(-power) * TOP)[None])
    out[0 : n * 16, :] = q.astype(jnp.int32).astype(jnp.int16).reshape(n * 16, WIDE)
    out[n * 16 : n * 16 + 16, :] = power.astype(jnp.int32).astype(jnp.int16)


def decode(ref):
    n = ref.shape[0] // 16 - 1
    power = ref[n * 16 : n * 16 + 16, :].astype(jnp.int32).astype(jnp.float32)
    q = ref[0 : n * 16, :].astype(jnp.int32).astype(jnp.float32).reshape(n, 16, WIDE)
    return (q * (jnp.exp2(power) * (1.0 / TOP))[None]).reshape(n * 16, WIDE)


def kernel(
    x_hbm, owners, occ_block, virt_block, occ_energy, virt,
    rows_out, mean_out,
    xv, w, keep, own, mid, last, snd1, rcv1, snd2, rcv2, snd3, rcv3, evec, ebuf,
    load_sem, s1s, s1r, s2s, s2r, s3s, s3r, es, er,
):
    aux = lax.axis_index("aux")
    pair = lax.axis_index("pair")
    z, x, y = aux // 8, (aux // 2) % 4, aux % 2
    hi, core = pair // 2, pair % 2

    def device(step, sign=1):
        dz, dx, dy, dh, dc = step
        turn = lambda at, by, n: lax.rem(at + sign * by + 2 * n, n)
        return (
            turn(z, dz, 4) * 8 + turn(x, dx, 4) * 2 + turn(y, dy, 2),
            turn(hi, dh, 2) * 2 + turn(core, dc, 2),
        )

    loads = []
    for i in range(4):
        part = pl.ds(i * 8, 8)
        c = pltpu.make_async_copy(x_hbm.at[part], xv.at[part], load_sem.at[i])
        c.start()
        loads.append(c)

    barrier = pltpu.get_barrier_semaphore()
    peers = FIRST_PEERS + SECOND_PEERS
    for s in peers:
        pl.semaphore_signal(barrier, inc=1, device_id=device(s, -1), device_id_type=MESH)

    def gap_row(u):
        return virt[pl.ds(virt_block[pair] * 4 + u % 4, 1), :] - occ_energy[occ_block[pair] * 8 + u // 4]

    own_gap = jnp.transpose(jnp.broadcast_to(gap_row(aux), (GROUP, GROUP)))
    owner_gap = [gap_row(owners[t]) for t in range(STEPS)]

    for c in loads:
        c.wait()
    for t in range(STEPS):
        w[t * GROUP : (t + 1) * GROUP, :] = xv[owners[t]]

    def partial(h, k):
        parts = []
        for dy in range(2):
            for j in range(4):
                dz, dx = (j, k) if h == 0 else (k, j)
                u = lax.rem(z + dz, 4) * 8 + lax.rem(x + dx, 4) * 2 + lax.rem(y + dy, 2)
                parts.append(xv[u, h * HALF : (h + 1) * HALF, :])
        rows = jnp.concatenate(parts, axis=0)
        return lax.dot_general(rows, w[...], (((1,), (1,)), ((), ())), preferred_element_type=jnp.float32)

    def copy(src, dst, ssem, rsem, step):
        return pltpu.make_async_remote_copy(
            src_ref=src, dst_ref=dst, send_sem=ssem, recv_sem=rsem,
            device_id=device(step), device_id_type=MESH,
        )

    X = ((0, 1, 0, 0, 0), (0, 3, 0, 0, 0))
    Z = ((1, 0, 0, 0, 0), (3, 0, 0, 0, 0))
    WAY = (1, 0, 0, 1, 0, 1)
    started = []

    def send(stage, h, m, v):
        snd, rcv, ssem, rsem = ((snd1, rcv1, s1s, s1r), (snd2, rcv2, s2s, s2r))[stage]
        axis = (X, Z)[(h + stage) % 2]
        i = h * 6 + m
        encode(v, snd.at[i])
        c = copy(snd.at[i], rcv.at[i], ssem.at[i], rsem.at[i], axis[WAY[m]])
        c.start()
        started.append(c)
        return c

    def arrived(stage, h, m, copies):
        copies[(stage, h, m)].wait_recv()
        return decode((rcv1, rcv2)[stage].at[h * 6 + m])

    copies = {}
    n1 = 4 * HALF
    pl.semaphore_wait(barrier, len(peers))

    for h in range(2):
        v = partial(h, 2)
        copies[(0, h, 0)] = send(0, h, 0, v[:n1])
        copies[(0, h, 1)] = send(0, h, 1, v[n1:])
    for h in range(2):
        v = partial(h, 1)
        copies[(0, h, 2)] = send(0, h, 2, v[:n1])
        keep[h, 0] = v[n1:]
        v = partial(h, 3)
        copies[(0, h, 3)] = send(0, h, 3, v[n1:])
        keep[h, 1] = v[:n1]
    for h in range(2):
        own[h] = partial(h, 0)
    for h in range(2):
        copies[(0, h, 4)] = send(0, h, 4, keep[h, 0] + arrived(0, h, 1, copies))
        copies[(0, h, 5)] = send(0, h, 5, keep[h, 1] + arrived(0, h, 0, copies))
    for h in range(2):
        own[h, :n1] += arrived(0, h, 2, copies)
        own[h, n1:] += arrived(0, h, 3, copies)
    for h in range(2):
        own[h, n1:] += arrived(0, h, 4, copies)
        own[h, :n1] += arrived(0, h, 5, copies)

    def block(h, dy, k):
        at = dy * n1 + k * HALF
        return own[h, at : at + HALF]

    for h in range(2):
        copies[(1, h, 0)] = send(1, h, 0, block(h, 0, 2))
        copies[(1, h, 1)] = send(1, h, 1, block(h, 1, 2))
        copies[(1, h, 2)] = send(1, h, 2, block(h, 0, 1))
        copies[(1, h, 3)] = send(1, h, 3, block(h, 1, 3))
    for h in range(2):
        copies[(1, h, 4)] = send(1, h, 4, block(h, 1, 1) + arrived(1, h, 1, copies))
        copies[(1, h, 5)] = send(1, h, 5, block(h, 0, 3) + arrived(1, h, 0, copies))
    for h in range(2):
        mid[h, 1] = block(h, 1, 0) + arrived(1, h, 3, copies)
        mid[h, 0] = block(h, 0, 0) + arrived(1, h, 2, copies)
    cross = []
    for h in range(2):
        encode(mid[h, 1] + arrived(1, h, 4, copies), snd3.at[h])
        c = copy(snd3.at[h], rcv3.at[h], s3s.at[h], s3r.at[h], (0, 0, 1, 0, 0))
        c.start()
        cross.append(c)
    for h in range(2):
        mid[h, 0] += arrived(1, h, 5, copies)
    for h in range(2):
        cross[h].wait_recv()
        whole = mid[h, 0] + decode(rcv3.at[h])
        terms = []
        for t in range(STEPS):
            v = whole[:, t * GROUP : (t + 1) * GROUP]
            gaps = own_gap[h * HALF : (h + 1) * HALF, :] + owner_gap[t]
            terms.append(v * v / gaps)
        last[h * HALF : (h + 1) * HALF, :] = terms[0] + terms[1]
    energy = jnp.sum(jnp.transpose(last[...]), axis=0, keepdims=True) * -spin_scale
    rows_out[...] = energy

    total = energy
    at = 0
    ecopies = []
    for stage, group in enumerate((FIRST_PEERS, SECOND_PEERS)):
        evec[stage] = jnp.broadcast_to(total, (8, GROUP))
        begin = at
        for s in group:
            c = copy(evec.at[stage], ebuf.at[at], es.at[at], er.at[at], s)
            c.start()
            ecopies.append(c)
            at += 1
        for i in range(begin, at):
            ecopies[i].wait_recv()
            total = total + ebuf[i, 0:1]
    mean = jnp.sum(total, axis=1, keepdims=True) * (1.0 / (4 * GROUPS * GROUP))
    mean_out[...] = mean
    for c in started + cross + ecopies:
        c.wait_send()


def shards(ia_aux, occ_block, virt_block, owners, occ_energy, virt_energy):
    smem = pl.BlockSpec(memory_space=pltpu.SMEM)
    vmem = pl.BlockSpec(memory_space=pltpu.VMEM)
    n1, n2 = 4 * HALF + 16, HALF + 16
    peers = len(FIRST_PEERS) + len(SECOND_PEERS)
    dma = lambda n: pltpu.SemaphoreType.DMA((n,))
    row_energy, mean = pl.pallas_call(
        kernel,
        out_shape=(
            jax.ShapeDtypeStruct((1, GROUP), jnp.float32),
            jax.ShapeDtypeStruct((1, 1), jnp.float32),
        ),
        in_specs=[pl.BlockSpec(memory_space=pl.ANY), smem, smem, smem, smem, vmem],
        out_specs=(vmem, vmem),
        scratch_shapes=[
            pltpu.VMEM((GROUPS, GROUP, DEPTH), jnp.bfloat16),
            pltpu.VMEM((WIDE, DEPTH), jnp.bfloat16),
            pltpu.VMEM((2, 2, 4 * HALF, WIDE), jnp.float32),
            pltpu.VMEM((2, 8 * HALF, WIDE), jnp.float32),
            pltpu.VMEM((2, 2, HALF, WIDE), jnp.float32),
            pltpu.VMEM((GROUP, GROUP), jnp.float32),
            pltpu.VMEM((12, n1, WIDE), jnp.int16),
            pltpu.VMEM((12, n1, WIDE), jnp.int16),
            pltpu.VMEM((12, n2, WIDE), jnp.int16),
            pltpu.VMEM((12, n2, WIDE), jnp.int16),
            pltpu.VMEM((2, n2, WIDE), jnp.int16),
            pltpu.VMEM((2, n2, WIDE), jnp.int16),
            pltpu.VMEM((2, 8, GROUP), jnp.float32),
            pltpu.VMEM((peers, 8, GROUP), jnp.float32),
            dma(4), dma(12), dma(12), dma(12), dma(12), dma(2), dma(2), dma(peers), dma(peers),
        ],
        compiler_params=pltpu.CompilerParams(
            collective_id=0, has_side_effects=True, vmem_limit_bytes=56 * 2**20
        ),
    )(
        ia_aux.reshape(GROUPS, GROUP, DEPTH),
        owners,
        occ_block,
        virt_block,
        occ_energy,
        virt_energy.reshape(-1, GROUP),
    )
    return row_energy.reshape(GROUP), mean.reshape(())


def solution(mesh):
    placed = (P("pair", "aux"), P(), P(), P(), P(), P())
    return jax.shard_map(
        shards, mesh=mesh, in_specs=placed, out_specs=(P(("pair", "aux")), P()), check_vma=False
    )
```

time: 264 us -> 45.4 us (0.17)
  waiting for transfers between devices: 139 us -> 0 us
  blocking collectives: 85.5 us -> 0 us
  Pallas kernels: 0 us -> 41.7 us
  between operations: 22.4 us -> 2.4 us
  matrix products: 6.57 us -> 0 us
  other arithmetic: 4.94 us -> 0 us
  local copies, waits for them, and re-layouts: 4.48 us -> 1.11 us
    reduce_scatter x1 -> x0, waiting for transfers between devices: 139 us -> none  [shards(): lax.psum_scatter(partial, 'aux', scatter_dimension=0, tiled=True)]
    psum x1 -> x0, blocking collectives: 85.5 us -> none  [shards(): window_total = lax.psum(jnp.sum(row_energy), ('aux', 'pair'))]
    pallas_call x0 -> x1, Pallas kernels: none -> 41.7 us  [shards(): pl.pallas_call(kernel, out_shape=(jax.ShapeDtypeStruct((1, GROUP), jnp.fl...]
    dot_general x1 -> x0, matrix products: 6.57 us -> none  [shards(): lax.dot_general(ia_aux, partners, (((1,), (1,)), ((), ())), preferred_ele...]
    dynamic_slice x3 -> x0, local copies, waits for them, and re-layouts: 3.16 us -> none  [the longest x1 1.43 us: row_gaps(): occ_energy[occ_index]]
    sub x1 -> x0, other arithmetic: 2.79 us -> none  [row_gaps(): lax.dynamic_slice_in_dim(virt_energy, virt_index, row_count)]
  transfers between devices with their start and end apart: 1 -> 0, of which waited for: 1 -> 0; matrix products, arithmetic and copies ran while one was open for 2% -> 0% of each run, Pallas kernels for 0% -> 0%
where the time goes in v2:
time: 45.4 us; the launch traced here: 45.2 us
  Pallas kernels  41.7 us (92%)
  between operations  2.4 us (5%)
  local copies, waits for them, and re-layouts  1.11 us (2%)
    pallas_call x1, Pallas kernels, shards(): pl.pallas_call(kernel, out_shape=(jax.ShapeDtypeStruct((1, GROUP), jnp.fl...  41.7 us
    unnamed x1, local copies, waits for them, and re-layouts  1.11 us

profile of v2, /device:TPU:1, one launch (start us, length us, event | category | flops | bytes accessed | tf_op | source)
XLA Modules:
  0.0 45.2 jit_solution(7133604160887157841)
XLA Ops:
  0.6 41.7 %shard_map.77 = (f32[1,128]{1,0:T(1,128)}, f32[1,1]{1,0:T(1,128)}) custom-call(bf16[32,128,768]{2,1,0:T(8,128)(2,1)} %bitcast.4, s32[2]{0:T(128)} %owners.1, s32[4]{0:T(128)} %occ_block.1, s32[4]{0:T(128)} %virt_block.1, f32[1200]{0:T(1024)} %occ_energy.1, f32[80,128]{1,0:T(8,128)} %bitcast.5), custom_call_target="tpu_custom_call" | custom-call | tf_op jit(solution)/shard_map/pallas_call | solution.py:209
  42.4 1.1 %copy.10 = f32[128]{0:T(128)} copy(f32[128]{0:T(128)} %bitcast.6) | data formatting | bytes 1024

commit v3 on v1

v3 whole, which is shorter than its diff:
```python
import itertools

import jax
import jax.numpy as jnp
from jax import lax
from jax.experimental import pallas as pl
from jax.experimental.pallas import tpu as pltpu
from jax.sharding import PartitionSpec as P

OB = 8
VB = 512
STEPS = 2
GROUP = 128
GROUPS = 32
HALF = GROUP // 2
WIDE = STEPS * GROUP
DEPTH = 768
TOP = 32764.0

MESH = pl.DeviceIdType.MESH
spin_scale = 1.3


def steps(*sizes):
    found = [s for s in itertools.product(*map(range, sizes)) if any(s)]
    return sorted(found, key=lambda s: -sum(min(a, n - a) for a, n in zip(s, (4, 4, 2, 2, 2))))


ENERGY_PEERS = (steps(1, 1, 1, 2, 2), steps(4, 4, 2, 1, 1))
ROW_PEERS = steps(4, 1, 2, 1, 1) + steps(1, 4, 2, 1, 1)
PEERS = ROW_PEERS[:0] + sorted(set(ROW_PEERS) | set(ENERGY_PEERS[0]))


def encode(v, out):
    v = v.reshape(-1, 16, WIDE)
    n = v.shape[0]
    halves = [v[:, :, t * GROUP : (t + 1) * GROUP] for t in range(STEPS)]
    top = jnp.maximum(*[jnp.max(jnp.abs(a), axis=0) for a in halves])
    power = jnp.ceil(jnp.log2(jnp.maximum(top, 1e-30)))
    scale = jnp.exp2(-power) * TOP
    for t, a in enumerate(halves):
        q = jnp.round(a * scale[None]).astype(jnp.int32).astype(jnp.int16)
        out[t * n * 16 : (t + 1) * n * 16, :] = q.reshape(n * 16, GROUP)
    out[STEPS * n * 16 : STEPS * n * 16 + 16, :] = power.astype(jnp.int32).astype(jnp.int16)


def decode(ref):
    rows = (ref.shape[0] - 16) // STEPS
    n = rows // 16
    power = ref[STEPS * rows : STEPS * rows + 16, :].astype(jnp.int32).astype(jnp.float32)
    scale = (jnp.exp2(power) * (1.0 / TOP))[None]
    halves = []
    for t in range(STEPS):
        q = ref[t * rows : (t + 1) * rows, :].astype(jnp.int32).astype(jnp.float32)
        halves.append((q.reshape(n, 16, GROUP) * scale).reshape(rows, GROUP))
    return jnp.concatenate(halves, axis=1)


def coded(rows):
    return STEPS * rows + 16


def loop(n, body):
    def step(i, carry):
        body(i)
        return carry

    lax.fori_loop(0, n, step, 0)


def kernel(
    x_hbm, owners_in, occ_block_in, virt_block_in, occ_energy_in, virt_in,
    rows_out, mean_out,
    owners, occ_block, virt_block, occ_energy, virt, xv, w, part, own_gap, last, evec, ebuf,
    snd1, rcv1, snd2, rcv2,
    load_sem, small_sem, es, er, s1, r1, s2, r2,
):
    aux = lax.axis_index("aux")
    pair = lax.axis_index("pair")
    z, x, y = aux // 8, (aux // 2) % 4, aux % 2
    hi, core = pair // 2, pair % 2

    def device(step, sign=1):
        dz, dx, dy, dh, dc = step
        turn = lambda at, by, n: lax.rem(at + sign * by + 2 * n, n)
        return (
            turn(z, dz, 4) * 8 + turn(x, dx, 4) * 2 + turn(y, dy, 2),
            turn(hi, dh, 2) * 2 + turn(core, dc, 2),
        )

    small = []
    for i, (a, b) in enumerate(
        ((owners_in, owners), (occ_block_in, occ_block), (virt_block_in, virt_block),
         (occ_energy_in, occ_energy), (virt_in, virt))
    ):
        small.append(pltpu.make_async_copy(a, b, small_sem.at[i]))
    loads = []
    for i in range(4):
        rows = pl.ds(i * 8, 8)
        loads.append(pltpu.make_async_copy(x_hbm.at[rows], xv.at[rows], load_sem.at[i]))
    barrier = pltpu.get_barrier_semaphore()
    for c in loads + small:
        c.start()
    for s in PEERS:
        pl.semaphore_signal(barrier, inc=1, device_id=device(s, -1), device_id_type=MESH)
    for c in small:
        c.wait()

    def gap_row(u):
        return virt[pl.ds(virt_block[pair] * 4 + u % 4, 1), :] - occ_energy[occ_block[pair] * 8 + u // 4]

    own_gap[...] = jnp.transpose(jnp.broadcast_to(gap_row(aux), (GROUP, GROUP)))
    owner_gap = [gap_row(owners[t]) for t in range(STEPS)]

    for c in loads:
        c.wait()
    for t in range(STEPS):
        w[t * GROUP : (t + 1) * GROUP, :] = xv[owners[t]].reshape(GROUP, DEPTH)

    def partial(h, k):
        parts = []
        for dy in range(2):
            for j in range(4):
                dz, dx = j * (1 - h) + k * h, k * (1 - h) + j * h
                u = lax.rem(z + dz, 4) * 8 + lax.rem(x + dx, 4) * 2 + lax.rem(y + dy, 2)
                parts.append(xv[u, h])
        rows = jnp.concatenate(parts, axis=0)
        v = lax.dot_general(rows, w[...], (((1,), (1,)), ((), ())), preferred_element_type=jnp.float32)
        part[h, k] = v.reshape(2, 2, 2, HALF, WIDE)

    def copy(src, dst, ssem, rsem, step):
        return pltpu.make_async_remote_copy(
            src_ref=src, dst_ref=dst, send_sem=ssem, recv_sem=rsem,
            device_id=device(step), device_id_type=MESH,
        )

    def post(dy, h, i, v, k):
        encode(v, snd1.at[dy, h, i])
        copy(
            snd1.at[dy, h, i], rcv1.at[dy, h, i], s1.at[dy, h, i], r1.at[dy, h, i],
            (k * h, k * (1 - h), 0, 0, 0),
        ).start()

    def take(dy, h, i):
        ref = rcv1.at[dy, h, i]
        pltpu.make_async_copy(ref, ref, r1.at[dy, h, i]).wait()
        return decode(ref)

    def side(h, k, dy, e):
        return part[h, k, dy, e].reshape(2 * HALF, WIDE)

    def far(dy, h, d):
        post(dy, h, d, side(h, 2, dy, d), 3 - 2 * d)

    def near(dy, h, d):
        post(dy, h, 2 + d, side(h, 1 + 2 * d, dy, d), 1 + 2 * d)

    def relay(dy, h, d):
        post(dy, h, 4 + d, side(h, 1 + 2 * d, dy, 1 - d) + take(dy, h, 1 - d), 1 + 2 * d)

    def gather(dy, h, e):
        v = side(h, 0, dy, e) + take(dy, h, 2 + e) + take(dy, h, 5 - e)
        part[h, 0, dy, e] = v.reshape(2, HALF, WIDE)

    def spread(dy, h, j):
        slot = j if dy else 3 + j
        encode(part[h, 0, dy, j // 2, j % 2], snd2.at[h, slot])
        copy(
            snd2.at[h, slot], rcv2.at[h, slot], s2.at[dy, h], r2.at[dy, h],
            (j * (1 - h), j * h, dy, 0, 0),
        ).start()

    def spread_wait(ref, sem, dy, h):
        here = ref.at[h, pl.ds(0, 4)] if dy else ref.at[h, pl.ds(4, 3)]
        pltpu.make_async_copy(here, here, sem.at[dy, h]).wait()

    def finish(h):
        spread_wait(rcv2, r2, 1, h)
        spread_wait(rcv2, r2, 0, h)
        whole = lax.fori_loop(0, 7, lambda i, v: v + decode(rcv2.at[h, i]), part[h, 0, 0, 0, 0])
        rows = pl.ds(pl.multiple_of(h * HALF, HALF), HALF)
        gaps = own_gap[rows, :]
        terms = []
        for t in range(STEPS):
            v = whole[:, t * GROUP : (t + 1) * GROUP]
            terms.append(v * v / (gaps + owner_gap[t]))
        last[rows, :] = terms[0] + terms[1]

    def close():
        def sent(i):
            dy, h, m = i // 12, (i // 6) % 2, i % 6
            ref = snd1.at[dy, h, m]
            pltpu.make_async_copy(ref, ref, s1.at[dy, h, m]).wait()

        loop(24, sent)
        for h in range(2):
            for dy in range(2):
                spread_wait(snd2, s2, dy, h)

    pairs = lambda f, dy: loop(4, lambda i: f(dy, i // 2, i % 2))

    def begin(h):
        partial(h, 2)
        loop(2, lambda d: far(1, h, d))

    def second(i):
        partial(i // 2, 1 + 2 * (i % 2))
        near(1, i // 2, i % 2)

    pl.semaphore_wait(barrier, len(PEERS))
    loop(2, begin)
    loop(4, second)
    pairs(far, 0)
    loop(2, lambda h: partial(h, 0))
    pairs(relay, 1)
    pairs(near, 0)
    pairs(relay, 0)
    pairs(gather, 1)
    loop(8, lambda i: spread(1, i % 2, lax.rem(i // 2 + 2, 4)))
    pairs(gather, 0)
    loop(6, lambda i: spread(0, i % 2, 1 + lax.rem(i // 2 + 1, 3)))
    loop(2, finish)

    energy = jnp.sum(jnp.transpose(last[...]), axis=0, keepdims=True) * -spin_scale
    rows_out[...] = energy
    total = energy
    at = 0
    for stage, group in enumerate(ENERGY_PEERS):
        evec[stage] = total
        here = ebuf.at[pl.ds(at, len(group))]
        for i, s in enumerate(group):
            copy(evec.at[stage], ebuf.at[at + i], es.at[stage], er.at[stage], s).start()
        pltpu.make_async_copy(here, here, er.at[stage]).wait()
        total = total + jnp.sum(here[...], axis=0)
        at += len(group)
    mean_out[...] = total
    close()
    at = 0
    for stage, group in enumerate(ENERGY_PEERS):
        here = ebuf.at[pl.ds(at, len(group))]
        pltpu.make_async_copy(here, here, es.at[stage]).wait()
        at += len(group)


def tail(rows, total, rows_out, mean_out):
    rows_out[...] = rows[...]
    mean_out[...] = jnp.sum(total[...], axis=1, keepdims=True) * (1.0 / (4 * GROUPS * GROUP))


def shards(ia_aux, occ_block, virt_block, owners, occ_energy, virt_energy):
    vmem = pl.BlockSpec(memory_space=pltpu.VMEM)
    peers = sum(map(len, ENERGY_PEERS))
    stages = len(ENERGY_PEERS)
    dma = lambda *n: pltpu.SemaphoreType.DMA(n)
    row = jax.ShapeDtypeStruct((1, GROUP), jnp.float32)
    row_energy, total = pl.pallas_call(
        kernel,
        out_shape=(row, row),
        in_specs=[pl.BlockSpec(memory_space=pl.ANY)] * 6,
        out_specs=(vmem, vmem),
        scratch_shapes=[
            pltpu.SMEM((STEPS,), jnp.int32),
            pltpu.SMEM(occ_block.shape, jnp.int32),
            pltpu.SMEM(virt_block.shape, jnp.int32),
            pltpu.SMEM(occ_energy.shape, jnp.float32),
            pltpu.VMEM((virt_energy.shape[0] // GROUP, GROUP), jnp.float32),
            pltpu.VMEM((GROUPS, 2, HALF, DEPTH), jnp.bfloat16),
            pltpu.VMEM((WIDE, DEPTH), jnp.bfloat16),
            pltpu.VMEM((2, 4, 2, 2, 2, HALF, WIDE), jnp.float32),
            pltpu.VMEM((GROUP, GROUP), jnp.float32),
            pltpu.VMEM((GROUP, GROUP), jnp.float32),
            pltpu.VMEM((stages, 1, GROUP), jnp.float32),
            pltpu.VMEM((peers, 1, GROUP), jnp.float32),
            pltpu.VMEM((2, 2, 6, coded(2 * HALF), GROUP), jnp.int16),
            pltpu.VMEM((2, 2, 6, coded(2 * HALF), GROUP), jnp.int16),
            pltpu.VMEM((2, 7, coded(HALF), GROUP), jnp.int16),
            pltpu.VMEM((2, 7, coded(HALF), GROUP), jnp.int16),
            dma(4), dma(5), dma(stages), dma(stages),
            dma(2, 2, 6), dma(2, 2, 6), dma(2, 2), dma(2, 2),
        ],
        compiler_params=pltpu.CompilerParams(
            collective_id=0, has_side_effects=True, vmem_limit_bytes=56 * 2**20
        ),
    )(
        ia_aux.reshape(GROUPS, 2, HALF, DEPTH),
        owners,
        occ_block,
        virt_block,
        occ_energy,
        virt_energy.reshape(-1, GROUP),
    )
    row_energy, mean = pl.pallas_call(
        tail, out_shape=(row, jax.ShapeDtypeStruct((1, 1), jnp.float32))
    )(row_energy, total)
    return row_energy.reshape(GROUP), mean.reshape(())


def solution(mesh):
    placed = (P("pair", "aux"), P(), P(), P(), P(), P())
    return jax.shard_map(
        shards, mesh=mesh, in_specs=placed, out_specs=(P(("pair", "aux")), P()), check_vma=False
    )
```

time: 264 us -> 37.3 us (0.14)
  waiting for transfers between devices: 139 us -> 0 us
  blocking collectives: 85.5 us -> 0 us
  Pallas kernels: 0 us -> 36.4 us
  between operations: 22.4 us -> 0.64 us
  matrix products: 6.57 us -> 0 us
  other arithmetic: 4.94 us -> 0 us
  local copies, waits for them, and re-layouts: 4.48 us -> 0 us
    reduce_scatter x1 -> x0, waiting for transfers between devices: 139 us -> none  [shards(): lax.psum_scatter(partial, 'aux', scatter_dimension=0, tiled=True)]
    psum x1 -> x0, blocking collectives: 85.5 us -> none  [shards(): window_total = lax.psum(jnp.sum(row_energy), ('aux', 'pair'))]
    pallas_call x0 -> x2, Pallas kernels: none -> 36.4 us  [the longest x1 35.1 us: shards(): pl.pallas_call(kernel, out_shape=(row, row), in_specs=[pl.BlockSpec(memor...]
    dot_general x1 -> x0, matrix products: 6.57 us -> none  [shards(): lax.dot_general(ia_aux, partners, (((1,), (1,)), ((), ())), preferred_ele...]
    dynamic_slice x3 -> x0, local copies, waits for them, and re-layouts: 3.16 us -> none  [the longest x1 1.43 us: row_gaps(): occ_energy[occ_index]]
    sub x1 -> x0, other arithmetic: 2.79 us -> none  [row_gaps(): lax.dynamic_slice_in_dim(virt_energy, virt_index, row_count)]
  transfers between devices with their start and end apart: 1 -> 0, of which waited for: 1 -> 0; matrix products, arithmetic and copies ran while one was open for 2% -> 0% of each run, Pallas kernels for 0% -> 0%
where the time goes in v3:
time: 37.3 us; the launch traced here: 37 us
  Pallas kernels  36.4 us (98%)
  between operations  0.64 us (2%)
    pallas_call x1, Pallas kernels, shards(): pl.pallas_call(kernel, out_shape=(row, row), in_specs=[pl.BlockSpec(memor...  35.1 us
    pallas_call x1, Pallas kernels, shards(): pl.pallas_call(tail, out_shape=(row, jax.ShapeDtypeStruct((1, 1), jnp.flo...  1.26 us

profile of v3, /device:TPU:1, one launch (start us, length us, event | category | flops | bytes accessed | tf_op | source)
XLA Modules:
  0.0 37.0 jit_solution(12585120151171396544)
XLA Ops:
  0.6 35.1 %shard_map.77 = (f32[1,128]{1,0:T(1,128)}, f32[1,128]{1,0:T(1,128)}) custom-call(bf16[32,2,64,768]{3,2,1,0:T(8,128)(2,1)} %bitcast.4, s32[2]{0:T(128)} %owners_in.1, s32[4]{0:T(128)} %occ_block_in.1, s32[4]{0:T(128)} %virt_block_in.1, f32[1200]{0:T(1024)} %occ_energy_in.1, f32[80,128]{1,0:T(8,128)} %bitcast.5), custom_call_target="tpu_custom_call" | custom-call | tf_op jit(solution)/shard_map/pallas_call | solution.py:256
  35.8 1.3 %shard_map.78 = (f32[1,128]{1,0:T(1,128)}, f32[1,1]{1,0:T(1,128)}) custom-call(f32[1,128]{1,0:T(1,128)} %get-tuple-element.6.rows, f32[1,128]{1,0:T(1,128)} %get-tuple-element.7.total), custom_call_target="tpu_custom_call" | custom-call | tf_op jit(solution)/shard_map/pallas_call | solution.py:292

commit v4 on v3

--- a/solution.py
+++ b/solution.py
@@ -19,16 +19,19 @@
 
 MESH = pl.DeviceIdType.MESH
 spin_scale = 1.3
+CHIPS = 64
 
 
 def steps(*sizes):
-    found = [s for s in itertools.product(*map(range, sizes)) if any(s)]
-    return sorted(found, key=lambda s: -sum(min(a, n - a) for a, n in zip(s, (4, 4, 2, 2, 2))))
-
-
-ENERGY_PEERS = (steps(1, 1, 1, 2, 2), steps(4, 4, 2, 1, 1))
-ROW_PEERS = steps(4, 1, 2, 1, 1) + steps(1, 4, 2, 1, 1)
-PEERS = ROW_PEERS[:0] + sorted(set(ROW_PEERS) | set(ENERGY_PEERS[0]))
+    return [s for s in itertools.product(*map(range, sizes)) if any(s)]
+
+
+OTHER_CORE = (0, 0, 0, 0, 1)
+OTHER_HALF = (0, 0, 0, 1, 0)
+CHIP_PEERS = sorted(
+    steps(4, 4, 2, 2, 1), key=lambda s: -sum(min(a, n - a) for a, n in zip(s, (4, 4, 2, 2, 2)))
+)
+PEERS = sorted(set(steps(4, 1, 2, 1, 1) + steps(1, 4, 2, 1, 1) + [OTHER_CORE, OTHER_HALF]))
 
 
 def encode(v, out):
@@ -70,10 +73,10 @@
 
 def kernel(
     x_hbm, owners_in, occ_block_in, virt_block_in, occ_energy_in, virt_in,
-    rows_out, mean_out,
+    rows_out, total_out,
     owners, occ_block, virt_block, occ_energy, virt, xv, w, part, own_gap, last, evec, ebuf,
     snd1, rcv1, snd2, rcv2,
-    load_sem, small_sem, es, er, s1, r1, s2, r2,
+    load_sem, small_sem, es, er, s1, r1, s2, r2, hello,
 ):
     aux = lax.axis_index("aux")
     pair = lax.axis_index("pair")
@@ -117,16 +120,15 @@
     for t in range(STEPS):
         w[t * GROUP : (t + 1) * GROUP, :] = xv[owners[t]].reshape(GROUP, DEPTH)
 
-    def partial(h, k):
+    def partial(h, k, dy):
         parts = []
-        for dy in range(2):
-            for j in range(4):
-                dz, dx = j * (1 - h) + k * h, k * (1 - h) + j * h
-                u = lax.rem(z + dz, 4) * 8 + lax.rem(x + dx, 4) * 2 + lax.rem(y + dy, 2)
-                parts.append(xv[u, h])
+        for j in range(4):
+            dz, dx = j * (1 - h) + k * h, k * (1 - h) + j * h
+            u = lax.rem(z + dz, 4) * 8 + lax.rem(x + dx, 4) * 2 + lax.rem(y + dy, 2)
+            parts.append(xv[u, h])
         rows = jnp.concatenate(parts, axis=0)
         v = lax.dot_general(rows, w[...], (((1,), (1,)), ((), ())), preferred_element_type=jnp.float32)
-        part[h, k] = v.reshape(2, 2, 2, HALF, WIDE)
+        part[h, k, dy] = v.reshape(2, 2, HALF, WIDE)
 
     def copy(src, dst, ssem, rsem, step):
         return pltpu.make_async_remote_copy(
@@ -174,10 +176,13 @@
         here = ref.at[h, pl.ds(0, 4)] if dy else ref.at[h, pl.ds(4, 3)]
         pltpu.make_async_copy(here, here, sem.at[dy, h]).wait()
 
+    def settle(h):
+        spread_wait(rcv2, r2, 1, h)
+        part[h, 0, 0, 0, 0] = lax.fori_loop(0, 4, lambda i, v: v + decode(rcv2.at[h, i]), part[h, 0, 0, 0, 0])
+
     def finish(h):
-        spread_wait(rcv2, r2, 1, h)
         spread_wait(rcv2, r2, 0, h)
-        whole = lax.fori_loop(0, 7, lambda i, v: v + decode(rcv2.at[h, i]), part[h, 0, 0, 0, 0])
+        whole = lax.fori_loop(4, 7, lambda i, v: v + decode(rcv2.at[h, i]), part[h, 0, 0, 0, 0])
         rows = pl.ds(pl.multiple_of(h * HALF, HALF), HALF)
         gaps = own_gap[rows, :]
         terms = []
@@ -199,47 +204,56 @@
 
     pairs = lambda f, dy: loop(4, lambda i: f(dy, i // 2, i % 2))
 
-    def begin(h):
-        partial(h, 2)
+    pl.semaphore_wait(barrier, len(PEERS))
+    for k in range(1, 4):
+        pl.semaphore_signal(hello.at[0], inc=1, device_id=device((0, k, 0, 0, 0)), device_id_type=MESH)
+    def first(h):
+        partial(h, 2, 1)
         loop(2, lambda d: far(1, h, d))
 
     def second(i):
-        partial(i // 2, 1 + 2 * (i % 2))
+        partial(i // 2, 1 + 2 * (i % 2), 1)
         near(1, i // 2, i % 2)
 
-    pl.semaphore_wait(barrier, len(PEERS))
-    loop(2, begin)
+    def third(h):
+        partial(h, 2, 0)
+        loop(2, lambda d: far(0, h, d))
+
+    loop(2, first)
     loop(4, second)
-    pairs(far, 0)
-    loop(2, lambda h: partial(h, 0))
+    loop(2, third)
+    pl.semaphore_wait(hello.at[0], 3)
+    pl.semaphore_signal(hello.at[1], inc=1, device_id=device(OTHER_HALF), device_id_type=MESH)
+    loop(4, lambda i: partial(i // 2, 1 + 2 * (i % 2), 0))
     pairs(relay, 1)
     pairs(near, 0)
+    loop(4, lambda i: partial(i // 2, 0, i % 2))
     pairs(relay, 0)
     pairs(gather, 1)
     loop(8, lambda i: spread(1, i % 2, lax.rem(i // 2 + 2, 4)))
     pairs(gather, 0)
     loop(6, lambda i: spread(0, i % 2, 1 + lax.rem(i // 2 + 1, 3)))
+    loop(2, settle)
     loop(2, finish)
-
-    energy = jnp.sum(jnp.transpose(last[...]), axis=0, keepdims=True) * -spin_scale
-    rows_out[...] = energy
-    total = energy
-    at = 0
-    for stage, group in enumerate(ENERGY_PEERS):
-        evec[stage] = total
-        here = ebuf.at[pl.ds(at, len(group))]
-        for i, s in enumerate(group):
-            copy(evec.at[stage], ebuf.at[at + i], es.at[stage], er.at[stage], s).start()
-        pltpu.make_async_copy(here, here, er.at[stage]).wait()
-        total = total + jnp.sum(here[...], axis=0)
-        at += len(group)
-    mean_out[...] = total
+    pl.semaphore_wait(hello.at[1], 1)
+
+    total = jnp.sum(last[...], axis=0, keepdims=True) * -spin_scale
+    evec[0] = total
+    swap = copy(evec.at[0], ebuf.at[CHIPS - 1], es.at[0], er.at[0], (0, 0, 0, 0, 1))
+    swap.start()
+    rows_out[...] = jnp.sum(jnp.transpose(last[...]), axis=0, keepdims=True) * -spin_scale
+    swap.wait_recv()
+    total = total + ebuf[CHIPS - 1]
+    evec[1] = total
+
+    for i, s in enumerate(CHIP_PEERS):
+        copy(evec.at[1], ebuf.at[i], es.at[1], er.at[1], s).start()
     close()
-    at = 0
-    for stage, group in enumerate(ENERGY_PEERS):
-        here = ebuf.at[pl.ds(at, len(group))]
-        pltpu.make_async_copy(here, here, es.at[stage]).wait()
-        at += len(group)
+    swap.wait_send()
+    here = ebuf.at[pl.ds(0, CHIPS - 1)]
+    pltpu.make_async_copy(here, here, es.at[1]).wait()
+    pltpu.make_async_copy(here, here, er.at[1]).wait()
+    total_out[...] = total + jnp.sum(here[...], axis=0)
 
 
 def tail(rows, total, rows_out, mean_out):
@@ -249,8 +263,6 @@
 
 def shards(ia_aux, occ_block, virt_block, owners, occ_energy, virt_energy):
     vmem = pl.BlockSpec(memory_space=pltpu.VMEM)
-    peers = sum(map(len, ENERGY_PEERS))
-    stages = len(ENERGY_PEERS)
     dma = lambda *n: pltpu.SemaphoreType.DMA(n)
     row = jax.ShapeDtypeStruct((1, GROUP), jnp.float32)
     row_energy, total = pl.pallas_call(
@@ -269,14 +281,14 @@
             pltpu.VMEM((2, 4, 2, 2, 2, HALF, WIDE), jnp.float32),
             pltpu.VMEM((GROUP, GROUP), jnp.float32),
             pltpu.VMEM((GROUP, GROUP), jnp.float32),
-            pltpu.VMEM((stages, 1, GROUP), jnp.float32),
-            pltpu.VMEM((peers, 1, GROUP), jnp.float32),
+            pltpu.VMEM((2, 1, GROUP), jnp.float32),
+            pltpu.VMEM((CHIPS, 1, GROUP), jnp.float32),
             pltpu.VMEM((2, 2, 6, coded(2 * HALF), GROUP), jnp.int16),
             pltpu.VMEM((2, 2, 6, coded(2 * HALF), GROUP), jnp.int16),
             pltpu.VMEM((2, 7, coded(HALF), GROUP), jnp.int16),
             pltpu.VMEM((2, 7, coded(HALF), GROUP), jnp.int16),
-            dma(4), dma(5), dma(stages), dma(stages),
-            dma(2, 2, 6), dma(2, 2, 6), dma(2, 2), dma(2, 2),
+            dma(4), dma(5), dma(2), dma(2),
+            dma(2, 2, 6), dma(2, 2, 6), dma(2, 2), dma(2, 2), pltpu.SemaphoreType.REGULAR((2,)),
         ],
         compiler_params=pltpu.CompilerParams(
             collective_id=0, has_side_effects=True, vmem_limit_bytes=56 * 2**20

time: 37.3 us -> 35.6 us (0.954)
  Pallas kernels: 36.4 us -> 34.9 us
    pallas_call x1, Pallas kernels: 35.1 us -> 33.6 us  [shards(): pl.pallas_call(kernel, out_shape=(row, row), in_specs=[pl.BlockSpec(memor...]
where the time goes in v4:
time: 35.6 us; the launch traced here: 35.5 us
  Pallas kernels  34.9 us (98%)
  between operations  0.64 us (2%)
    pallas_call x1, Pallas kernels, shards(): pl.pallas_call(kernel, out_shape=(row, row), in_specs=[pl.BlockSpec(memor...  33.6 us
    pallas_call x1, Pallas kernels, shards(): pl.pallas_call(tail, out_shape=(row, jax.ShapeDtypeStruct((1, 1), jnp.flo...  1.26 us

profile of v4, /device:TPU:1, one launch (start us, length us, event | category | flops | bytes accessed | tf_op | source)
XLA Modules:
  0.0 35.5 jit_solution(15168685947201812048)
XLA Ops:
  0.6 33.6 %shard_map.77 = (f32[1,128]{1,0:T(1,128)}, f32[1,128]{1,0:T(1,128)}) custom-call(bf16[32,2,64,768]{3,2,1,0:T(8,128)(2,1)} %bitcast.4, s32[2]{0:T(128)} %owners_in.1, s32[4]{0:T(128)} %occ_block_in.1, s32[4]{0:T(128)} %virt_block_in.1, f32[1200]{0:T(1024)} %occ_energy_in.1, f32[80,128]{1,0:T(8,128)} %bitcast.5), custom_call_target="tpu_custom_call" | custom-call | tf_op jit(solution)/shard_map/pallas_call | solution.py:268
  34.2 1.3 %shard_map.78 = (f32[1,128]{1,0:T(1,128)}, f32[1,1]{1,0:T(1,128)}) custom-call(f32[1,128]{1,0:T(1,128)} %get-tuple-element.6.rows, f32[1,128]{1,0:T(1,128)} %get-tuple-element.7.total), custom_call_target="tpu_custom_call" | custom-call | tf_op jit(solution)/shard_map/pallas_call | solution.py:304

commit v5 on v4

--- a/solution.py
+++ b/solution.py
@@ -19,7 +19,6 @@
 
 MESH = pl.DeviceIdType.MESH
 spin_scale = 1.3
-CHIPS = 64
 
 
 def steps(*sizes):
@@ -28,9 +27,17 @@
 
 OTHER_CORE = (0, 0, 0, 0, 1)
 OTHER_HALF = (0, 0, 0, 1, 0)
-CHIP_PEERS = sorted(
-    steps(4, 4, 2, 2, 1), key=lambda s: -sum(min(a, n - a) for a, n in zip(s, (4, 4, 2, 2, 2)))
-)
+
+
+def hops(s):
+    return sum(min(a, n - a) for a, n in zip(s, (4, 4, 2, 2, 2)))
+
+
+CHIP_PEERS = sorted(steps(4, 4, 2, 2, 1), key=lambda s: -hops(s))
+FAR = 0
+FAR_CHIPS = [s for s in CHIP_PEERS if hops(s) >= FAR]
+NEAR_CHIPS = [s for s in CHIP_PEERS if hops(s) < FAR]
+SUMS = 2 * len(FAR_CHIPS) + len(NEAR_CHIPS)
 PEERS = sorted(set(steps(4, 1, 2, 1, 1) + steps(1, 4, 2, 1, 1) + [OTHER_CORE, OTHER_HALF]))
 
 
@@ -83,13 +90,17 @@
     z, x, y = aux // 8, (aux // 2) % 4, aux % 2
     hi, core = pair // 2, pair % 2
 
-    def device(step, sign=1):
+    zs = [((z + i) % 4) * 8 for i in range(4)]
+    xs = [((x + i) % 4) * 2 for i in range(4)]
+    ys = [y, 1 - y]
+    his = [hi * 2, 2 - hi * 2]
+    cores = [core, 1 - core]
+
+    def device(step):
         dz, dx, dy, dh, dc = step
-        turn = lambda at, by, n: lax.rem(at + sign * by + 2 * n, n)
-        return (
-            turn(z, dz, 4) * 8 + turn(x, dx, 4) * 2 + turn(y, dy, 2),
-            turn(hi, dh, 2) * 2 + turn(core, dc, 2),
-        )
+        at = zs[dz] if isinstance(dz, int) else ((z + dz) % 4) * 8
+        at = at + (xs[dx] if isinstance(dx, int) else ((x + dx) % 4) * 2)
+        return at + (ys[dy] if isinstance(dy, int) else (y + dy) % 2), his[dh] + cores[dc]
 
     small = []
     for i, (a, b) in enumerate(
@@ -105,7 +116,7 @@
     for c in loads + small:
         c.start()
     for s in PEERS:
-        pl.semaphore_signal(barrier, inc=1, device_id=device(s, -1), device_id_type=MESH)
+        pl.semaphore_signal(barrier, inc=1, device_id=device(s), device_id_type=MESH)
     for c in small:
         c.wait()
 
@@ -124,7 +135,7 @@
         parts = []
         for j in range(4):
             dz, dx = j * (1 - h) + k * h, k * (1 - h) + j * h
-            u = lax.rem(z + dz, 4) * 8 + lax.rem(x + dx, 4) * 2 + lax.rem(y + dy, 2)
+            u = ((z + dz) % 4) * 8 + ((x + dx) % 4) * 2 + ((y + dy) % 2)
             parts.append(xv[u, h])
         rows = jnp.concatenate(parts, axis=0)
         v = lax.dot_general(rows, w[...], (((1,), (1,)), ((), ())), preferred_element_type=jnp.float32)
@@ -229,28 +240,32 @@
     pairs(near, 0)
     loop(4, lambda i: partial(i // 2, 0, i % 2))
     pairs(relay, 0)
+    pl.semaphore_wait(hello.at[1], 1)
+    pl.semaphore_signal(hello.at[2], inc=1, device_id=device(OTHER_CORE), device_id_type=MESH)
     pairs(gather, 1)
     loop(8, lambda i: spread(1, i % 2, lax.rem(i // 2 + 2, 4)))
     pairs(gather, 0)
     loop(6, lambda i: spread(0, i % 2, 1 + lax.rem(i // 2 + 1, 3)))
     loop(2, settle)
     loop(2, finish)
-    pl.semaphore_wait(hello.at[1], 1)
+    pl.semaphore_wait(hello.at[2], 1)
 
     total = jnp.sum(last[...], axis=0, keepdims=True) * -spin_scale
     evec[0] = total
-    swap = copy(evec.at[0], ebuf.at[CHIPS - 1], es.at[0], er.at[0], (0, 0, 0, 0, 1))
+    swap = copy(evec.at[0], ebuf.at[SUMS], es.at[0], er.at[0], OTHER_CORE)
     swap.start()
+    for i, s in enumerate(FAR_CHIPS):
+        for c in range(2):
+            copy(evec.at[0], ebuf.at[2 * i + c], es.at[1], er.at[1], s[:4] + (c,)).start()
+    swap.wait_recv()
+    total = total + ebuf[SUMS]
+    evec[1] = total
+    for i, s in enumerate(NEAR_CHIPS):
+        copy(evec.at[1], ebuf.at[2 * len(FAR_CHIPS) + i], es.at[1], er.at[1], s).start()
     rows_out[...] = jnp.sum(jnp.transpose(last[...]), axis=0, keepdims=True) * -spin_scale
-    swap.wait_recv()
-    total = total + ebuf[CHIPS - 1]
-    evec[1] = total
-
-    for i, s in enumerate(CHIP_PEERS):
-        copy(evec.at[1], ebuf.at[i], es.at[1], er.at[1], s).start()
     close()
     swap.wait_send()
-    here = ebuf.at[pl.ds(0, CHIPS - 1)]
+    here = ebuf.at[pl.ds(0, SUMS)]
     pltpu.make_async_copy(here, here, es.at[1]).wait()
     pltpu.make_async_copy(here, here, er.at[1]).wait()
     total_out[...] = total + jnp.sum(here[...], axis=0)
@@ -267,7 +282,7 @@
     row = jax.ShapeDtypeStruct((1, GROUP), jnp.float32)
     row_energy, total = pl.pallas_call(
         kernel,
-        out_shape=(row, row),
+        out_shape=(pltpu.VMEM((1, GROUP), jnp.float32), pltpu.VMEM((1, GROUP), jnp.float32)),
         in_specs=[pl.BlockSpec(memory_space=pl.ANY)] * 6,
         out_specs=(vmem, vmem),
         scratch_shapes=[
@@ -282,13 +297,13 @@
             pltpu.VMEM((GROUP, GROUP), jnp.float32),
             pltpu.VMEM((GROUP, GROUP), jnp.float32),
             pltpu.VMEM((2, 1, GROUP), jnp.float32),
-            pltpu.VMEM((CHIPS, 1, GROUP), jnp.float32),
+            pltpu.VMEM((SUMS + 1, 1, GROUP), jnp.float32),
             pltpu.VMEM((2, 2, 6, coded(2 * HALF), GROUP), jnp.int16),
             pltpu.VMEM((2, 2, 6, coded(2 * HALF), GROUP), jnp.int16),
             pltpu.VMEM((2, 7, coded(HALF), GROUP), jnp.int16),
             pltpu.VMEM((2, 7, coded(HALF), GROUP), jnp.int16),
             dma(4), dma(5), dma(2), dma(2),
-            dma(2, 2, 6), dma(2, 2, 6), dma(2, 2), dma(2, 2), pltpu.SemaphoreType.REGULAR((2,)),
+            dma(2, 2, 6), dma(2, 2, 6), dma(2, 2), dma(2, 2), pltpu.SemaphoreType.REGULAR((3,)),
         ],
         compiler_params=pltpu.CompilerParams(
             collective_id=0, has_side_effects=True, vmem_limit_bytes=56 * 2**20
@@ -301,8 +316,9 @@
         occ_energy,
         virt_energy.reshape(-1, GROUP),
     )
+    row_energy, total = (pltpu.with_memory_space_constraint(a, pltpu.VMEM) for a in (row_energy, total))
     row_energy, mean = pl.pallas_call(
-        tail, out_shape=(row, jax.ShapeDtypeStruct((1, 1), jnp.float32))
+        tail, out_shape=(row, jax.ShapeDtypeStruct((1, 1), jnp.float32)), in_specs=[vmem, vmem]
     )(row_energy, total)
     return row_energy.reshape(GROUP), mean.reshape(())
 

time: 35.6 us -> 34.2 us (0.961)
  Pallas kernels: 34.9 us -> 33.4 us
    pallas_call x1, Pallas kernels: 33.6 us -> 32.8 us  [shards(): pl.pallas_call(kernel, out_shape=(pltpu.VMEM((1, GROUP), jnp.float32), pl...]
    pallas_call x1, Pallas kernels: 1.26 us -> 0.59 us  [shards(): pl.pallas_call(tail, out_shape=(row, jax.ShapeDtypeStruct((1, 1), jnp.flo...]
where the time goes in v5:
time: 34.2 us; the launch traced here: 34.1 us
  Pallas kernels  33.4 us (98%)
  between operations  0.64 us (2%)
    pallas_call x1, Pallas kernels, shards(): pl.pallas_call(kernel, out_shape=(pltpu.VMEM((1, GROUP), jnp.float32), pl...  32.8 us

profile of v5, /device:TPU:1, one launch (start us, length us, event | category | flops | bytes accessed | tf_op | source)
XLA Modules:
  0.0 34.1 jit_solution(498076343291955257)
XLA Ops:
  0.6 32.8 %shard_map.77 = (f32[1,128]{1,0:T(1,128)S(1)}, f32[1,128]{1,0:T(1,128)S(1)}) custom-call(bf16[32,2,64,768]{3,2,1,0:T(8,128)(2,1)} %bitcast.4, s32[2]{0:T(128)} %owners_in.1, s32[4]{0:T(128)} %occ_block_in.1, s32[4]{0:T(128)} %virt_block_in.1, f32[1200]{0:T(1024)} %occ_energy_in.1, f32[80,128]{1,0:T(8,128)} %bitcast.5), custom_call_target="tpu_custom_call" | custom-call | tf_op jit(solution)/shard_map/pallas_call | solution.py:283
  33.5 0.6 %shard_map.78 = (f32[1,128]{1,0:T(1,128)}, f32[1,1]{1,0:T(1,128)}) custom-call(f32[1,128]{1,0:T(1,128)S(1)} %get-tuple-element.6.rows, f32[1,128]{1,0:T(1,128)S(1)} %get-tuple-element.7.total), custom_call_target="tpu_custom_call" | custom-call | tf_op jit(solution)/shard_map/pallas_call | solution.py:320

commit v6 on v5

--- a/solution.py
+++ b/solution.py
@@ -33,11 +33,7 @@
     return sum(min(a, n - a) for a, n in zip(s, (4, 4, 2, 2, 2)))
 
 
-CHIP_PEERS = sorted(steps(4, 4, 2, 2, 1), key=lambda s: -hops(s))
-FAR = 0
-FAR_CHIPS = [s for s in CHIP_PEERS if hops(s) >= FAR]
-NEAR_CHIPS = [s for s in CHIP_PEERS if hops(s) < FAR]
-SUMS = 2 * len(FAR_CHIPS) + len(NEAR_CHIPS)
+ALL_PEERS = sorted(steps(4, 4, 2, 2, 2), key=lambda s: -hops(s))
 PEERS = sorted(set(steps(4, 1, 2, 1, 1) + steps(1, 4, 2, 1, 1) + [OTHER_CORE, OTHER_HALF]))
 
 
@@ -81,7 +77,7 @@
 def kernel(
     x_hbm, owners_in, occ_block_in, virt_block_in, occ_energy_in, virt_in,
     rows_out, total_out,
-    owners, occ_block, virt_block, occ_energy, virt, xv, w, part, own_gap, last, evec, ebuf,
+    owners, occ_block, virt_block, occ_energy, virt, xv, w, part, inverse, last, evec, ebuf,
     snd1, rcv1, snd2, rcv2,
     load_sem, small_sem, es, er, s1, r1, s2, r2, hello,
 ):
@@ -123,8 +119,9 @@
     def gap_row(u):
         return virt[pl.ds(virt_block[pair] * 4 + u % 4, 1), :] - occ_energy[occ_block[pair] * 8 + u // 4]
 
-    own_gap[...] = jnp.transpose(jnp.broadcast_to(gap_row(aux), (GROUP, GROUP)))
-    owner_gap = [gap_row(owners[t]) for t in range(STEPS)]
+    own_gap = jnp.transpose(jnp.broadcast_to(gap_row(aux), (GROUP, GROUP)))
+    for t in range(STEPS):
+        inverse[t] = 1.0 / (own_gap + gap_row(owners[t]))
 
     for c in loads:
         c.wait()
@@ -189,17 +186,16 @@
 
     def settle(h):
         spread_wait(rcv2, r2, 1, h)
-        part[h, 0, 0, 0, 0] = lax.fori_loop(0, 4, lambda i, v: v + decode(rcv2.at[h, i]), part[h, 0, 0, 0, 0])
+        part[h, 0, 0, 0, 0] = part[h, 0, 0, 0, 0] + sum(decode(rcv2.at[h, i]) for i in range(4))
 
     def finish(h):
         spread_wait(rcv2, r2, 0, h)
-        whole = lax.fori_loop(4, 7, lambda i, v: v + decode(rcv2.at[h, i]), part[h, 0, 0, 0, 0])
-        rows = pl.ds(pl.multiple_of(h * HALF, HALF), HALF)
-        gaps = own_gap[rows, :]
+        whole = part[h, 0, 0, 0, 0] + sum(decode(rcv2.at[h, i]) for i in range(4, 7))
+        rows = pl.ds(h * HALF, HALF)
         terms = []
         for t in range(STEPS):
             v = whole[:, t * GROUP : (t + 1) * GROUP]
-            terms.append(v * v / (gaps + owner_gap[t]))
+            terms.append(v * v * inverse[t, rows, :])
         last[rows, :] = terms[0] + terms[1]
 
     def close():
@@ -215,9 +211,6 @@
 
     pairs = lambda f, dy: loop(4, lambda i: f(dy, i // 2, i % 2))
 
-    pl.semaphore_wait(barrier, len(PEERS))
-    for k in range(1, 4):
-        pl.semaphore_signal(hello.at[0], inc=1, device_id=device((0, k, 0, 0, 0)), device_id_type=MESH)
     def first(h):
         partial(h, 2, 1)
         loop(2, lambda d: far(1, h, d))
@@ -230,7 +223,12 @@
         partial(h, 2, 0)
         loop(2, lambda d: far(0, h, d))
 
-    loop(2, first)
+    partial(0, 2, 1)
+    partial(1, 2, 1)
+    pl.semaphore_wait(barrier, len(PEERS))
+    pairs(far, 1)
+    for k in range(1, 4):
+        pl.semaphore_signal(hello.at[0], inc=1, device_id=device((0, k, 0, 0, 0)), device_id_type=MESH)
     loop(4, second)
     loop(2, third)
     pl.semaphore_wait(hello.at[0], 3)
@@ -246,29 +244,21 @@
     loop(8, lambda i: spread(1, i % 2, lax.rem(i // 2 + 2, 4)))
     pairs(gather, 0)
     loop(6, lambda i: spread(0, i % 2, 1 + lax.rem(i // 2 + 1, 3)))
-    loop(2, settle)
-    loop(2, finish)
+    for h in range(2):
+        settle(h)
+    for h in range(2):
+        finish(h)
     pl.semaphore_wait(hello.at[2], 1)
 
     total = jnp.sum(last[...], axis=0, keepdims=True) * -spin_scale
-    evec[0] = total
-    swap = copy(evec.at[0], ebuf.at[SUMS], es.at[0], er.at[0], OTHER_CORE)
-    swap.start()
-    for i, s in enumerate(FAR_CHIPS):
-        for c in range(2):
-            copy(evec.at[0], ebuf.at[2 * i + c], es.at[1], er.at[1], s[:4] + (c,)).start()
-    swap.wait_recv()
-    total = total + ebuf[SUMS]
-    evec[1] = total
-    for i, s in enumerate(NEAR_CHIPS):
-        copy(evec.at[1], ebuf.at[2 * len(FAR_CHIPS) + i], es.at[1], er.at[1], s).start()
+    evec[...] = total
+    for i, s in enumerate(ALL_PEERS):
+        copy(evec, ebuf.at[i], es, er, s).start()
     rows_out[...] = jnp.sum(jnp.transpose(last[...]), axis=0, keepdims=True) * -spin_scale
     close()
-    swap.wait_send()
-    here = ebuf.at[pl.ds(0, SUMS)]
-    pltpu.make_async_copy(here, here, es.at[1]).wait()
-    pltpu.make_async_copy(here, here, er.at[1]).wait()
-    total_out[...] = total + jnp.sum(here[...], axis=0)
+    pltpu.make_async_copy(ebuf, ebuf, es).wait()
+    pltpu.make_async_copy(ebuf, ebuf, er).wait()
+    total_out[...] = total + jnp.sum(ebuf[...], axis=0)
 
 
 def tail(rows, total, rows_out, mean_out):
@@ -278,7 +268,7 @@
 
 def shards(ia_aux, occ_block, virt_block, owners, occ_energy, virt_energy):
     vmem = pl.BlockSpec(memory_space=pltpu.VMEM)
-    dma = lambda *n: pltpu.SemaphoreType.DMA(n)
+    dma = lambda *n: pltpu.SemaphoreType.DMA(n) if n else pltpu.SemaphoreType.DMA
     row = jax.ShapeDtypeStruct((1, GROUP), jnp.float32)
     row_energy, total = pl.pallas_call(
         kernel,
@@ -294,15 +284,15 @@
             pltpu.VMEM((GROUPS, 2, HALF, DEPTH), jnp.bfloat16),
             pltpu.VMEM((WIDE, DEPTH), jnp.bfloat16),
             pltpu.VMEM((2, 4, 2, 2, 2, HALF, WIDE), jnp.float32),
+            pltpu.VMEM((STEPS, GROUP, GROUP), jnp.float32),
             pltpu.VMEM((GROUP, GROUP), jnp.float32),
-            pltpu.VMEM((GROUP, GROUP), jnp.float32),
-            pltpu.VMEM((2, 1, GROUP), jnp.float32),
-            pltpu.VMEM((SUMS + 1, 1, GROUP), jnp.float32),
+            pltpu.VMEM((1, GROUP), jnp.float32),
+            pltpu.VMEM((len(ALL_PEERS), 1, GROUP), jnp.float32),
             pltpu.VMEM((2, 2, 6, coded(2 * HALF), GROUP), jnp.int16),
             pltpu.VMEM((2, 2, 6, coded(2 * HALF), GROUP), jnp.int16),
             pltpu.VMEM((2, 7, coded(HALF), GROUP), jnp.int16),
             pltpu.VMEM((2, 7, coded(HALF), GROUP), jnp.int16),
-            dma(4), dma(5), dma(2), dma(2),
+            dma(4), dma(5), dma(), dma(),
             dma(2, 2, 6), dma(2, 2, 6), dma(2, 2), dma(2, 2), pltpu.SemaphoreType.REGULAR((3,)),
         ],
         compiler_params=pltpu.CompilerParams(

time: 34.2 us -> 33.6 us (0.982)
  Pallas kernels: 33.4 us -> 32.9 us
    pallas_call x1, Pallas kernels: 32.8 us -> 32.3 us  [shards(): pl.pallas_call(kernel, out_shape=(pltpu.VMEM((1, GROUP), jnp.float32), pl...]
where the time goes in v6:
time: 33.6 us; the launch traced here: 33.5 us
  Pallas kernels  32.9 us (98%)
  between operations  0.64 us (2%)
    pallas_call x1, Pallas kernels, shards(): pl.pallas_call(kernel, out_shape=(pltpu.VMEM((1, GROUP), jnp.float32), pl...  32.3 us

profile of v6, /device:TPU:1, one launch (start us, length us, event | category | flops | bytes accessed | tf_op | source)
XLA Modules:
  0.0 33.5 jit_solution(9136901841535455346)
XLA Ops:
  0.6 32.3 %shard_map.77 = (f32[1,128]{1,0:T(1,128)S(1)}, f32[1,128]{1,0:T(1,128)S(1)}) custom-call(bf16[32,2,64,768]{3,2,1,0:T(8,128)(2,1)} %bitcast.4, s32[2]{0:T(128)} %owners_in.1, s32[4]{0:T(128)} %occ_block_in.1, s32[4]{0:T(128)} %virt_block_in.1, f32[1200]{0:T(1024)} %occ_energy_in.1, f32[80,128]{1,0:T(8,128)} %bitcast.5), custom_call_target="tpu_custom_call" | custom-call | tf_op jit(solution)/shard_map/pallas_call | solution.py:273
  32.9 0.6 %shard_map.78 = (f32[1,128]{1,0:T(1,128)}, f32[1,1]{1,0:T(1,128)}) custom-call(f32[1,128]{1,0:T(1,128)S(1)} %get-tuple-element.6.rows, f32[1,128]{1,0:T(1,128)S(1)} %get-tuple-element.7.total), custom_call_target="tpu_custom_call" | custom-call | tf_op jit(solution)/shard_map/pallas_call | solution.py:310

commit v7 on v6

--- a/solution.py
+++ b/solution.py
@@ -240,10 +240,12 @@
     pairs(relay, 0)
     pl.semaphore_wait(hello.at[1], 1)
     pl.semaphore_signal(hello.at[2], inc=1, device_id=device(OTHER_CORE), device_id_type=MESH)
-    pairs(gather, 1)
-    loop(8, lambda i: spread(1, i % 2, lax.rem(i // 2 + 2, 4)))
-    pairs(gather, 0)
-    loop(6, lambda i: spread(0, i % 2, 1 + lax.rem(i // 2 + 1, 3)))
+    for h in range(2):
+        loop(2, lambda e: gather(1, h, e))
+        loop(4, lambda i: spread(1, h, lax.rem(i + 2, 4)))
+    for h in range(2):
+        loop(2, lambda e: gather(0, h, e))
+        loop(3, lambda i: spread(0, h, 1 + lax.rem(i + 1, 3)))
     for h in range(2):
         settle(h)
     for h in range(2):

time: 33.6 us -> 33.1 us (0.985)
  Pallas kernels: 32.9 us -> 32.4 us
    pallas_call x1, Pallas kernels: 32.3 us -> 31.8 us  [shards(): pl.pallas_call(kernel, out_shape=(pltpu.VMEM((1, GROUP), jnp.float32), pl...]
where the time goes in v7:
time: 33.1 us; the launch traced here: 33 us
  Pallas kernels  32.4 us (98%)
  between operations  0.64 us (2%)
    pallas_call x1, Pallas kernels, shards(): pl.pallas_call(kernel, out_shape=(pltpu.VMEM((1, GROUP), jnp.float32), pl...  31.8 us

profile of v7, /device:TPU:1, one launch (start us, length us, event | category | flops | bytes accessed | tf_op | source)
XLA Modules:
  0.0 33.0 jit_solution(1990217740914411962)
XLA Ops:
  0.6 31.8 %shard_map.77 = (f32[1,128]{1,0:T(1,128)S(1)}, f32[1,128]{1,0:T(1,128)S(1)}) custom-call(bf16[32,2,64,768]{3,2,1,0:T(8,128)(2,1)} %bitcast.4, s32[2]{0:T(128)} %owners_in.1, s32[4]{0:T(128)} %occ_block_in.1, s32[4]{0:T(128)} %virt_block_in.1, f32[1200]{0:T(1024)} %occ_energy_in.1, f32[80,128]{1,0:T(8,128)} %bitcast.5), custom_call_target="tpu_custom_call" | custom-call | tf_op jit(solution)/shard_map/pallas_call | solution.py:275
  32.4 0.6 %shard_map.78 = (f32[1,128]{1,0:T(1,128)}, f32[1,1]{1,0:T(1,128)}) custom-call(f32[1,128]{1,0:T(1,128)S(1)} %get-tuple-element.6.rows, f32[1,128]{1,0:T(1,128)S(1)} %get-tuple-element.7.total), custom_call_target="tpu_custom_call" | custom-call | tf_op jit(solution)/shard_map/pallas_call | solution.py:312
